TPU v7x, 128 devices: a whole 4x4x4 slice. The times are simulated.
128 devices in a mesh: ex: 32 (over z, y, x_hi), eig: 4 (over x_lo, core).
Axes of the slice: x: 4 (x_hi: 2, x_lo: 2; x = x_hi * 2 + x_lo), y: 4, z: 4, core: 2. Of those that a mesh axis runs over, the one named last changes fastest.
Arguments:
- layer_inputs: bfloat16 [4096, 14336], P('ex', 'eig'), may hold values from -6 to 6
- out_grads: bfloat16 [4096, 4096], P('eig'), may hold values from -6 to 6
- hidden_basis: bfloat16 [14336, 14336], P('eig', 'ex'), may hold values from -0.046875 to 0.046875
- output_basis: bfloat16 [4096, 4096], P(None, 'ex'), may hold values from -0.09375 to 0.09375
- eigenvalues: float32 [4096, 14336], P(None, 'ex'), may hold values from 1920 to 192000
- query_inputs: bfloat16 [32, 8, 14336], P('ex'), may hold values from -6 to 6
- query_grads: bfloat16 [32, 8, 4096], P('ex'), may hold values from -6 to 6
- query_owner: int32 [4], replicated, may hold values from 0 to 31
- example_lengths: int32 [32, 4], replicated, may hold values from 1 to 64, 128 in all within a row
Outputs:
- token_scores: float32 [4, 4096], P(None, ('eig', 'ex'))
- example_scores: float32 [4, 128], P(None, ('eig', 'ex'))
Inputs may be any that keep to these rules, and one draw needn't show every extreme that they name: `example_lengths`: each shard's 4 lengths sum to 128.
All inputs are finite; a program needn't handle non-finite values.
Results may differ from a plain program's by a relative error of at most 0.025.
Values may be sent and summed in bfloat16 or wider, within the bound.
No kernel may reach another device: no remote copies, remote signals or barrier semaphores. Data moves between devices by JAX's collectives and lax.ppermute only.
A program may use at most 192 MiB of HBM per device.

v0:
```python
import functools

import jax
import jax.numpy as jnp
import numpy as np
from jax import lax
from jax.experimental import pallas as pl
from jax.experimental.pallas import tpu as pltpu
from jax.sharding import Mesh, PartitionSpec as P

DAMP = 480
AXES = ("z", "y", "xh", "xl", "c")
SIZES = (4, 4, 2, 2, 2)


def permutation(move):
    pairs = []
    for source, place in enumerate(np.ndindex(*SIZES)):
        target = tuple(a % b for a, b in zip(move(*place), SIZES))
        pairs.append((source, int(np.ravel_multi_index(target, SIZES))))
    return pairs


RING_Z = permutation(lambda z, y, xh, xl, c: (z + 1 - 2 * c, y, xh, xl, c))
RING_Y = permutation(lambda z, y, xh, xl, c: (z, y + 1 - 2 * c, xh, xl, c))
OTHER_XH = permutation(lambda z, y, xh, xl, c: (z, y, xh + 1, xl, c))
OTHER_XL = permutation(lambda z, y, xh, xl, c: (z, y, xh, xl + 1, c))
OTHER_CORE = permutation(lambda z, y, xh, xl, c: (z, y, xh, xl, c + 1))
NEXT_XH = permutation(lambda z, y, xh, xl, c: (z, y, xh + 1, xl + 1, c))


def send(value, pairs):
    return lax.ppermute(value, AXES, pairs)


def after(done, later):
    return lax.optimization_barrier((done, later))


def dot(a, b):
    return jnp.dot(a, b, preferred_element_type=jnp.float32)


def precond_kernel(at, *refs):
    near, far, grads = refs[0:4], refs[4:8], refs[8:12]
    inputs, out = refs[12:]
    x = pl.program_id(1)
    block = grads[0].shape[0]
    for k in range(4):
        inv = jnp.where(x == 0, near[k][...], far[k][...]).astype(jnp.float32).T
        for q in range(out.shape[1]):
            outer = dot(grads[k][...], inputs[0, q])
            out[0, q, k * block : (k + 1) * block, :] = (outer * inv).astype(
                jnp.bfloat16
            )


def precond_of(places, near, far, grads, inputs):
    _, queries, depth, width = inputs.shape
    units = near.shape[1]
    block = units // 16
    blocks = places.shape[0] // 2

    def columns(k):
        return pl.BlockSpec((width, block), lambda s, x, at: (0, at[4 * s + k]))

    def lines(k):
        return pl.BlockSpec((block, depth), lambda s, x, at: (at[4 * s + k], 0))

    return pl.pallas_call(
        precond_kernel,
        grid_spec=pltpu.PrefetchScalarGridSpec(
            num_scalar_prefetch=1,
            grid=(blocks // 4, 2),
            in_specs=[columns(k) for k in range(4)]
            + [columns(blocks + k) for k in range(4)]
            + [lines(k) for k in range(4)]
            + [
                pl.BlockSpec(
                    (1, queries, depth, width), lambda s, x, at: (x, 0, 0, 0)
                )
            ],
            out_specs=pl.BlockSpec(
                (1, queries, 4 * block, width),
                lambda s, x, at: (x, 0, s, 0),
            ),
        ),
        out_shape=jax.ShapeDtypeStruct(
            (2, queries, blocks * block, width), jnp.bfloat16
        ),
        compiler_params=pltpu.CompilerParams(vmem_limit_bytes=18 * 1024 * 1024),
        cost_estimate=pl.CostEstimate(
            flops=2 * 2 * blocks * block * depth * width * queries,
            bytes_accessed=5_000_000 * blocks,
            transcendentals=0,
        ),
    )(places, *[near] * 4, *[far] * 4, *[grads] * 4, inputs)


def mixed_kernel(chunks, *refs):
    steps, preconds, before = refs[:chunks], refs[chunks : 2 * chunks], refs[2 * chunks : -2]
    out, wide = refs[-2:]
    block = steps[0].shape[-1]

    @pl.when((pl.program_id(0) == 0) & (pl.program_id(1) == 0))
    def _():
        for s in range(chunks):
            for n in range(4):
                wide[s, :, n * block : (n + 1) * block] = steps[s][n]

    total = before[0][0, 0].astype(jnp.float32) if before else 0.0
    for s in range(chunks):
        total += dot(wide[s], preconds[s][0, 0])
    out[0, 0] = total.astype(jnp.bfloat16)


def mixed_of(steps, precond, start, *before):
    _, queries, units, width = precond.shape
    _, tokens, block = steps[0].shape
    chunks = len(steps)
    each = pl.BlockSpec((1, 1, tokens, width), lambda x, q: (x, q, 0, 0))

    def chunk(s):
        return pl.BlockSpec((1, 1, units // 4, width), lambda x, q: (x, q, s, 0))

    return pl.pallas_call(
        functools.partial(mixed_kernel, chunks),
        grid=(2, queries),
        in_specs=[
            pl.BlockSpec(
                (4, tokens, block), lambda x, q: (0, 0, 0), pipeline_mode=pl.Buffered(1)
            )
        ]
        * chunks
        + [chunk(start + s) for s in range(chunks)]
        + [each] * len(before),
        out_specs=each,
        out_shape=jax.ShapeDtypeStruct((2, queries, tokens, width), jnp.bfloat16),
        scratch_shapes=[pltpu.VMEM((chunks, tokens, units // 4), jnp.bfloat16)],
        compiler_params=pltpu.CompilerParams(vmem_limit_bytes=24 * 1024 * 1024),
        cost_estimate=pl.CostEstimate(
            flops=chunks * queries * tokens * units * width,
            bytes_accessed=10_000_000 * chunks,
            transcendentals=0,
        ),
    )(*steps, *[precond] * chunks, *before)


def products_kernel(at, rows, basis, out):
    made = lax.dot_general(
        rows[...],
        basis[...],
        (((1,), (1,)), ((), ())),
        preferred_element_type=jnp.float32,
    )
    out[0] = made.astype(jnp.bfloat16)


def products_of(z_blocks, gathered, basis):
    groups = z_blocks.shape[0]
    width, depth = basis.shape
    tokens = gathered.shape[0] // 4
    part = tokens // 2
    out = pl.pallas_call(
        products_kernel,
        grid_spec=pltpu.PrefetchScalarGridSpec(
            num_scalar_prefetch=1,
            grid=(groups, 2),
            in_specs=[
                pl.BlockSpec((part, depth), lambda g, r, at: (2 * at[g] + r, 0)),
                pl.BlockSpec(
                    (width, depth), lambda g, r, at: (0, 0), pipeline_mode=pl.Buffered(1)
                ),
            ],
            out_specs=pl.BlockSpec((1, part, width), lambda g, r, at: (g, r, 0)),
        ),
        out_shape=jax.ShapeDtypeStruct((groups, tokens, width), jnp.bfloat16),
        compiler_params=pltpu.CompilerParams(vmem_limit_bytes=52 * 1024 * 1024),
        cost_estimate=pl.CostEstimate(
            flops=2 * groups * tokens * depth * width,
            bytes_accessed=4_000_000 * groups,
            transcendentals=0,
        ),
    )(z_blocks, gathered, basis)
    return [out[g] for g in range(groups)]


def score_kernel(mixed, stay, stay_far, arrived, arrived_far, out):
    hidden = []
    for a, b in ((stay, arrived), (stay_far, arrived_far)):
        both = a[...].astype(jnp.float32) + b[...].astype(jnp.float32)
        hidden.append(both.astype(jnp.bfloat16).astype(jnp.float32))
    for q in range(out.shape[0]):
        terms = sum(mixed[x, q].astype(jnp.float32) * hidden[x] for x in range(2))
        out[q, :] = jnp.sum(terms, axis=-1)


def scores_of(mixed, stay, arrived):
    _, queries, tokens, width = mixed.shape
    rows = 128
    part = pl.BlockSpec((rows, width), lambda t: (t, 0))
    return pl.pallas_call(
        score_kernel,
        grid=(tokens // rows,),
        in_specs=[pl.BlockSpec((2, queries, rows, width), lambda t: (0, 0, t, 0))]
        + [part] * 4,
        out_specs=pl.BlockSpec((queries, rows), lambda t: (0, t)),
        out_shape=jax.ShapeDtypeStruct((queries, tokens), jnp.float32),
        compiler_params=pltpu.CompilerParams(vmem_limit_bytes=16 * 1024 * 1024),
        cost_estimate=pl.CostEstimate(
            flops=4 * queries * tokens * width,
            bytes_accessed=6_000_000,
            transcendentals=0,
        ),
    )(mixed, *stay, *arrived)


def per_device(
    layer_inputs,
    out_grads,
    hidden_basis,
    output_basis,
    eigenvalues,
    query_inputs,
    query_grads,
    query_owner,
    example_lengths,
):
    z, y, xh, xl, c = (lax.axis_index(name) for name in AXES)
    way = 1 - 2 * c
    tokens = layer_inputs.shape[0]
    width = hidden_basis.shape[1]
    units = out_grads.shape[1]
    queries = query_owner.shape[0]
    qtok = query_inputs.shape[1]
    ex, plane = ("z", "y", "xh"), ("z", "y")

    slot = jnp.concatenate([query_inputs[0], query_grads[0]], axis=-1)
    slot_far = send(slot, OTHER_XH)
    grads = dot(out_grads, output_basis).astype(jnp.bfloat16).reshape(4, 2, tokens, -1)
    grads_kept = lax.dynamic_index_in_dim(grads, xh, axis=1, keepdims=False)
    grads_far = send(
        lax.dynamic_index_in_dim(grads, 1 - xh, axis=1, keepdims=False), OTHER_XH
    )
    gathered = lax.all_gather(layer_inputs, plane, axis=0, tiled=True)
    inverse = (1.0 / (eigenvalues.T + DAMP)).astype(jnp.bfloat16)
    grads_far, inverse = after(grads_far, inverse)
    part = units // 2
    mine = lax.dynamic_slice_in_dim(inverse, c * part, part, axis=1)
    eigen_half = send(mine, NEXT_XH)

    pair = jnp.where(
        xh == 0,
        jnp.concatenate([grads_kept, grads_far], axis=-1),
        jnp.concatenate([grads_far, grads_kept], axis=-1),
    ).reshape(4 * tokens, -1)
    near_z = [pair, send(pair, RING_Z)]
    near_z[1], (slot, slot_far) = after(near_z[1], (slot, slot_far))
    near_z.append(send(near_z[-1], RING_Z))
    near_z.append(send(near_z[-1], RING_Z))

    slots = jnp.where(
        xh == 0, jnp.stack([slot, slot_far]), jnp.stack([slot_far, slot])
    )
    columns = slots[..., : 16 * 2 * width].reshape(2, qtok, 16, 2 * width)
    of_grads = slots[..., 16 * 2 * width :].reshape(2, qtok, 16, units // 16)
    slots = jnp.concatenate([columns, of_grads], axis=-1).transpose(2, 0, 1, 3)
    slots = lax.all_to_all(slots, plane, 0, 0, tiled=True)
    (slots, eigen_half, near_z[2]), basis = after(
        (slots, eigen_half, near_z[2]), hidden_basis
    )
    owned = jnp.take(slots.reshape(32, qtok, -1), query_owner, axis=0)
    owner_grads = lax.all_to_all(
        jnp.broadcast_to(
            owned[None, ..., 2 * width :], (16, queries, qtok, units // 16)
        ),
        plane,
        0,
        0,
        tiled=True,
    )
    owner_grads = owner_grads.transpose(0, 3, 1, 2).reshape(units, queries * qtok)
    owned = owned[..., : 2 * width].reshape(queries, qtok, 2, width)
    owned = owned.transpose(2, 0, 1, 3)
    owned = jnp.where(xh == 0, owned, owned[::-1])
    owner_inputs = jnp.where(
        jnp.eye(queries, dtype=jnp.bool_)[:, :, None, None], owned[:, None], 0
    ).reshape(2, queries, queries * qtok, width)

    basis_far = send(basis, OTHER_XH)
    near_z[3], owner_grads = lax.optimization_barrier((near_z[3], owner_grads))
    steps = [jnp.stack(near_z)]
    steps.append(send(steps[0], RING_Y))
    eigen_other = send(eigen_half, OTHER_CORE)
    inverse_far = jnp.concatenate([eigen_half, eigen_other], axis=1)

    def precond(chunks):
        places = [
            (z - way * jnp.arange(4)) % 4 * 4 + (y - way * s) % 4 for s in chunks
        ]
        places = jnp.concatenate(places).astype(jnp.int32)
        return precond_of(
            jnp.concatenate([places, (places + 8 * c) % 16]),
            inverse,
            inverse_far,
            owner_grads,
            owner_inputs,
        )

    preconds = precond((0, 1, 2, 3))
    early = mixed_of(steps[:1], preconds, 0)
    early, preconds, steps[1] = lax.optimization_barrier((early, preconds, steps[1]))
    steps.append(send(steps[1], RING_Y))


    def swapped(values, pairs):
        return [send(v, pairs) for v in values]

    def total(one, two):
        return [
            (a.astype(jnp.float32) + b.astype(jnp.float32)).astype(jnp.bfloat16)
            for a, b in zip(one, two)
        ]

    z_blocks = 2 * jnp.stack([1 - xl, 1 - xl, xl, xl]) + jnp.stack([1 - c, c] * 2)
    z_blocks = z_blocks.astype(jnp.int32)
    made = products_of(z_blocks, gathered, hidden_basis.T)
    made, basis_far, steps[2] = lax.optimization_barrier((made, basis_far, steps[2]))
    steps.append(send(steps[2], RING_Y))
    made_far = products_of(z_blocks[:2], gathered, basis_far.T)
    made_far, steps[3], gathered = lax.optimization_barrier(
        (made_far, steps[3], gathered)
    )
    made_far += products_of(z_blocks[2:], gathered, basis_far.T)
    there, here, there_last, here_last = zip(made, made_far)
    leave = total(here, swapped(there, OTHER_CORE))
    arrived = swapped(leave, OTHER_XL)
    stay = total(here_last, swapped(there_last, OTHER_CORE))
    steps[3], early, leave, stay = lax.optimization_barrier(
        (steps[3], early, leave, stay)
    )
    mixed = mixed_of(steps[1:], preconds, 1, early)
    mixed, arrived = lax.optimization_barrier((mixed, arrived))
    scores = scores_of(mixed, stay, arrived)
    scores = scores.reshape(queries, 4, tokens)

    full = jnp.broadcast_to(
        scores.transpose(1, 0, 2)[:, None, None], (4, 4, 2, queries, tokens)
    )
    meant = (jnp.arange(4) // 2 == xh)[None, :, None, None, None]
    full = jnp.where(meant, full, 0.0).reshape(32, queries, tokens)
    terms = lax.all_to_all(full, ex, 0, 0, tiled=True)
    shard_scores = jnp.sum(terms, axis=0)

    index = 2 * (y % 2) + xh
    per_out = tokens // 4
    token_out = lax.dynamic_slice_in_dim(shard_scores, index * per_out, per_out, 1)
    shard = 8 * (2 * xl + c) + 2 * z + y // 2
    lengths = lax.dynamic_index_in_dim(example_lengths, shard, axis=0, keepdims=False)
    at = jnp.arange(lengths.shape[0])
    start = jnp.sum(jnp.where(at < index, lengths, 0))
    end = jnp.sum(jnp.where(at <= index, lengths, 0))
    position = jnp.arange(tokens)
    inside = (position >= start) & (position < end)
    example_out = jnp.sum(jnp.where(inside, shard_scores, 0.0), axis=1, keepdims=True)
    return token_out, example_out


def solution(mesh):
    fine = Mesh(mesh.devices.reshape(SIZES), AXES)
    ex, eig = ("z", "y", "xh"), ("xl", "c")
    placed = (
        P(ex, eig),
        P(eig, None),
        P(eig, ex),
        P(None, ex),
        P(None, ex),
        P(ex, None, None),
        P(ex, None, None),
        P(),
        P(),
    )
    out = P(None, eig + ex)
    return jax.shard_map(
        per_device, mesh=fine, in_specs=placed, out_specs=(out, out), check_vma=False
    )
```

profile of v0, /device:TPU:0, one launch (start us, length us, event | category | flops | bytes accessed | tf_op | source)
XLA Modules:
  0.0 219.0 jit_solution(56368181150309440)
XLA Ops:
  7.2 0.7 all-gather.2.cloned.1.call-update
  7.9 0.5 copy-done
  8.4 5.9 %convolution_convert_fusion = bf16[1024,128]{1,0:T(8,128)(2,1)S(1)} fusion(bf16[1024,4096]{1,0:T(8,128)(2,1)} %param.10, bf16[4096,128]{1,0:T(8,128)(2,1)S(1)} %copy-done), kind=kOutput, calls=%fused_computation.4 | convolution fusion | flops 1073872896 | bytes 9699328 | tf_op jit(solution)/shard_map/dot_general | solution.py:41
  14.3 3.2 %collective-permute-start = (bf16[4,128,128]{2,1,0:T(8,128)(2,1)S(1)}, bf16[4,128,128]{2,1,0:T(8,128)(2,1)S(1)}, u32[]{:S(2)}, u32[]{:S(2)}) collective-permute-start(bf16[4,128,128]{2,1,0:T(8,128)(2,1)S(1)} %get-tuple-element.75), channel_id=1, source_target_pairs={{0,4},{1,5},{2,6},{3,7},{4,0},{5,1},{6,2},{7,3},{8,12},{9,13},{10,... | collective-permute-start | bytes 393224 | tf_op jit(solution)/shard_map/ppermute | solution.py:33
  17.5 0.5 collective-permute-start.2
  18.0 2.8 %fusion.refs_0_.refs_1_.refs_2_.refs_3_ = bf16[448,4096]{1,0:T(8,128)(2,1)} fusion(f32[4096,448]{0,1:T(8,128)S(1)} %copy-done.5), kind=kLoop, calls=%fused_computation.3 | loop fusion | flops 5505024 | bytes 11010048 | tf_op jit(solution)/shard_map/convert_element_type | solution.py:246
  20.8 0.6 collective-permute-done
  21.4 0.1 maximum_select_fusion.2
  21.5 2.0 collective-permute-start.1
  23.5 1.8 constant_dynamic-slice_fusion.1
  25.3 3.6 %collective-permute-start.3 = (bf16[448,2048]{1,0:T(8,128)(2,1)S(1)}, bf16[448,2048]{1,0:T(8,128)(2,1)}, u32[]{:S(2)}, u32[]{:S(2)}) collective-permute-start(bf16[448,2048]{1,0:T(8,128)(2,1)S(1)} %constant_dynamic-slice_fusion.1), channel_id=1, source_target_pairs={{0,6},{1,7},{2,4},{3,5},{4,2},{5,3},{6,0},{7,1},{8,14},{9,15},{10,... | collective-permute-start | bytes 5505032 | tf_op jit(solution)/shard_map/ppermute | solution.py:33
  28.9 6.0 %collective-permute-done.1 = bf16[512,256]{1,0:T(8,128)(2,1)S(1)} collective-permute-done((bf16[512,256]{1,0:T(8,128)(2,1)S(1)}, bf16[512,256]{1,0:T(8,128)(2,1)S(1)}, u32[]{:S(2)}, u32[]{:S(2)}) %collective-permute-start.1) | collective-permute-done | bytes 262176 | tf_op jit(solution)/shard_map/ppermute | solution.py:33
  34.9 0.7 copy-done.6
  35.6 1.2 maximum_select_fusion
  37.0 0.9 copy.46
  37.9 6.4 %all-to-all-start = ((bf16[16,2,8,1152]{3,2,1,0:T(8,128)(2,1)}), bf16[16,2,8,1152]{3,2,1,0:T(8,128)(2,1)S(1)}, u32[]{:S(2)}, u32[]{:S(2)}) async-start(bf16[16,2,8,1152]{3,2,1,0:T(8,128)(2,1)} %copy.46), calls=%async_computation | async-start | bytes 1179648 | tf_op jit(solution)/shard_map/all_to_all | solution.py:268
  44.3 1.9 collective-permute-start.4
  46.3 14.1 %collective-permute-done.4 = bf16[512,256]{1,0:T(8,128)(2,1)} collective-permute-done((bf16[512,256]{1,0:T(8,128)(2,1)}, bf16[512,256]{1,0:T(8,128)(2,1)}, u32[]{:S(2)}, u32[]{:S(2)}) %collective-permute-start.4) | collective-permute-done | bytes 262176 | tf_op jit(solution)/shard_map/ppermute | solution.py:33
  60.4 8.8 %collective-permute-done.3 = bf16[448,2048]{1,0:T(8,128)(2,1)} collective-permute-done((bf16[448,2048]{1,0:T(8,128)(2,1)S(1)}, bf16[448,2048]{1,0:T(8,128)(2,1)}, u32[]{:S(2)}, u32[]{:S(2)}) %collective-permute-start.3) | collective-permute-done | bytes 1835040 | tf_op jit(solution)/shard_map/ppermute | solution.py:33
  69.5 0.1 broadcast_in_dim.93
  69.7 2.7 %collective-permute-start.8 = (bf16[3584,448]{0,1:T(8,128)(2,1)}, bf16[3584,448]{0,1:T(8,128)(2,1)}, u32[]{:S(2)}, u32[]{:S(2)}) collective-permute-start(bf16[3584,448]{0,1:T(8,128)(2,1)} %param.11), channel_id=1, source_target_pairs={{0,4},{1,5},{2,6},{3,7},{4,0},{5,1},{6,2},{7,3},{8,12},{9,13},{10,... | collective-permute-start | bytes 9633800 | tf_op jit(solution)/shard_map/ppermute | solution.py:33
  72.3 0.6 gather_fusion
  73.0 0.7 broadcast_in_dim.91
  73.7 7.6 %all-to-all-start.1 = ((bf16[16,4,8,256]{3,2,1,0:T(8,128)(2,1)}), bf16[16,4,8,256]{3,2,1,0:T(8,128)(2,1)S(1)}, u32[]{:S(2)}, u32[]{:S(2)}) async-start(bf16[16,4,8,256]{3,2,1,0:T(8,128)(2,1)} %broadcast_in_dim.91), calls=%async_computation.1 | async-start | bytes 524288 | tf_op jit(solution)/shard_map/all_to_all | solution.py:273
  81.3 0.1 maximum_select_fusion.1
  81.4 0.1 reshape.125
  81.6 0.4 rev.3
  82.1 11.4 %all-to-all-done.1 = bf16[16,4,8,256]{3,2,1,0:T(8,128)(2,1)S(1)} async-done(((bf16[16,4,8,256]{3,2,1,0:T(8,128)(2,1)}), bf16[16,4,8,256]{3,2,1,0:T(8,128)(2,1)S(1)}, u32[]{:S(2)}, u32[]{:S(2)}) %all-to-all-start.1) | async-done | bytes 262176 | tf_op jit(solution)/shard_map/all_to_all | solution.py:273
  93.5 0.1 copy.64
  93.6 0.8 copy.59
  94.4 1.1 pad_maximum_fusion.1.refs_0_
  95.5 0.6 collective-permute-start.7
  96.2 1.4 copy.49.refs_8_.refs_9_.refs_10_.refs_11_
  97.7 2.8 %pad_maximum_fusion.refs_4_.refs_5_.refs_6_.refs_7_ = bf16[448,4096]{1,0:T(8,128)(2,1)S(1)} fusion(bf16[448,2048]{1,0:T(8,128)(2,1)} %collective-permute-done.6, bf16[448,2048]{1,0:T(8,128)(2,1)} %collective-permute-done.3), kind=kLoop, calls=%fused_computation.2 | loop fusion | flops 7340032 | bytes 7340032 | tf_op jit(solution)/shard_map/concatenate | solution.py:295
  100.4 0.6 copy-done.2
  101.1 16.1 %shard_map.104.refs_1_.refs_3_.refs_4_.refs_5_ = bf16[2,4,4096,448]{3,2,1,0:T(8,128)(2,1)} custom-call(s32[32]{0:T(128)S(1)} %concatenate.61.at, bf16[448,4096]{1,0:T(8,128)(2,1)S(1)} %copy-done.2, bf16[448,4096]{1,0:T(8,128)(2,1)S(1)} %copy-done.2, bf16[448,4096]{1,0:T(8,128)(2,1)S(1)} %copy-done.2, bf16[448,4096]{1,0:T(8,128)(2,1)S(1)} %copy-done.2, ...), custom_call_target="tpu_custom_call" | custom-call | flops 939524096 | bytes 80000000 | tf_op jit(solution)/shard_map/pallas_call | solution.py:70
  117.1 8.9 %shard_map.105.refs_6_ = bf16[2,4,512,448]{3,2,1,0:T(8,128)(2,1)S(1)} custom-call(bf16[4,512,256]{2,1,0:T(8,128)(2,1)S(1)} %pad_maximum_fusion.1.refs_0_, bf16[2,4,4096,448]{3,2,1,0:T(8,128)(2,1)} %shard_map.104.refs_1_.refs_3_.refs_4_.refs_5_), custom_call_target="tpu_custom_call" | custom-call | flops 3758096384 | bytes 10000000 | tf_op jit(solution)/shard_map/pallas_call | solution.py:126
  126.0 1.9 copy-done.3
  128.0 0.9 collective-permute-done.7.refs_0_
  129.0 0.1 broadcast_in_dim.86
  129.2 0.2 dynamic-slice_reduce_fusion
  129.4 0.6 fusion.4
  130.0 14.5 %shard_map.106 = bf16[4,512,448]{2,1,0:T(8,128)(2,1)} custom-call(s32[4]{0:T(128)S(1)} %fusion.8.at, bf16[2048,3584]{1,0:T(8,128)(2,1)} %all-gather.2.cloned.1.call-done.rows, bf16[448,3584]{1,0:T(8,128)(2,1)} %bitcast.96), custom_call_target="tpu_custom_call" | custom-call | flops 6576668672 | bytes 16000000 | tf_op jit(solution)/shard_map/pallas_call | solution.py:164
  144.5 1.7 slice_bitcast_fusion.4
  146.2 0.8 collective-permute-start.10
  147.1 0.5 collective-permute-start.13
  147.6 8.1 %shard_map.107 = bf16[2,512,448]{2,1,0:T(8,128)(2,1)S(1)} custom-call(s32[2]{0:T(128)S(1)} %get-tuple-element.77.at, bf16[2048,3584]{1,0:T(8,128)(2,1)} %all-gather.2.cloned.1.call-done.rows, bf16[448,3584]{1,0:T(8,128)(2,1)} %bitcast.28.basis), custom_call_target="tpu_custom_call" | custom-call | flops 3288334336 | bytes 8000000 | tf_op jit(solution)/shard_map/pallas_call | solution.py:164
  155.8 0.1 add_convert_fusion.2
  155.9 1.5 collective-permute-start.15
  157.5 4.8 %collective-permute-done.10.refs_2_ = bf16[4,512,256]{2,1,0:T(8,128)(2,1)S(1)} collective-permute-done((bf16[4,512,256]{2,1,0:T(8,128)(2,1)S(1)}, bf16[4,512,256]{2,1,0:T(8,128)(2,1)S(1)}, u32[]{:S(2)}, u32[]{:S(2)}) %collective-permute-start.10) | collective-permute-done | bytes 1048608 | tf_op jit(solution)/shard_map/ppermute | solution.py:33
  162.3 8.1 %shard_map.108 = bf16[2,512,448]{2,1,0:T(8,128)(2,1)S(1)} custom-call(s32[2]{0:T(128)S(1)} %get-tuple-element.76.at, bf16[2048,3584]{1,0:T(8,128)(2,1)} %all-gather.2.cloned.1.call-done.rows, bf16[448,3584]{1,0:T(8,128)(2,1)} %bitcast.28.basis), custom_call_target="tpu_custom_call" | custom-call | flops 3288334336 | bytes 8000000 | tf_op jit(solution)/shard_map/pallas_call | solution.py:164
  170.4 0.6 collective-permute-start.14
  171.0 0.1 add_convert_fusion.stay
  171.1 0.1 add_convert_fusion.1
  171.3 1.5 collective-permute-start.16
  172.8 0.1 fusion.1.stay_far
  173.0 17.0 %shard_map.109.mixed = bf16[2,4,512,448]{3,2,1,0:T(8,128)(2,1)S(1)} custom-call(bf16[4,512,256]{2,1,0:T(8,128)(2,1)S(1)} %collective-permute-done.7.refs_0_, bf16[4,512,256]{2,1,0:T(8,128)(2,1)S(1)} %collective-permute-done.9.refs_1_, bf16[4,512,256]{2,1,0:T(8,128)(2,1)S(1)} %collective-permute-done.10.refs_2_, ...), custom_call_target="tpu_custom_call" | custom-call | flops 11274289152 | bytes 30000000 | tf_op jit(solution)/shard_map/pallas_call | solution.py:126
  190.0 1.8 shard_map.110
  191.8 0.7 bitcast_select_fusion
  192.6 8.4 %all-to-all-start.2 = ((f32[32,4,128]{2,1,0:T(4,128)}), f32[32,4,128]{2,1,0:T(4,128)S(1)}, u32[]{:S(2)}, u32[]{:S(2)}) async-start(f32[32,4,128]{2,1,0:T(4,128)} %bitcast_select_fusion), calls=%async_computation.2 | async-start | bytes 131072 | tf_op jit(solution)/shard_map/all_to_all | solution.py:352
  201.0 1.3 compare_and_fusion
  202.3 8.6 %all-to-all-done.2 = f32[32,4,128]{2,1,0:T(4,128)S(1)} async-done(((f32[32,4,128]{2,1,0:T(4,128)}), f32[32,4,128]{2,1,0:T(4,128)S(1)}, u32[]{:S(2)}, u32[]{:S(2)}) %all-to-all-start.2) | async-done | bytes 65568 | tf_op jit(solution)/shard_map/all_to_all | solution.py:352
  210.9 0.7 constant_dynamic-slice_fusion
  211.5 0.6 select_reduce_fusion
  (69 shorter events, 1.4 us)
Async XLA Ops:
  7.2 1.2 copy-start
  7.2 122.8 %all-gather.2.cloned.1.call-start = ((), (), s32[]{:S(2)}) async-start(), calls=%async_computation.3 | async-start | bytes 15597568 | tf_op jit(solution)/shard_map/all_gather | solution.py:245
  8.4 9.1 %copy-start.8 = (bf16[1,8,14336]{2,1,0:T(8,128)(2,1)S(1)}, bf16[1,8,14336]{2,1,0:T(8,128)(2,1)}, u32[]{:S(2)}) copy-start(bf16[1,8,14336]{2,1,0:T(8,128)(2,1)} %param.14) | copy-start | bytes 688132
  8.4 9.1 %copy-start.9 = (bf16[1,8,4096]{2,1,0:T(8,128)(2,1)S(1)}, bf16[1,8,4096]{2,1,0:T(8,128)(2,1)}, u32[]{:S(2)}) copy-start(bf16[1,8,4096]{2,1,0:T(8,128)(2,1)} %param.15) | copy-start | bytes 196612
  8.4 9.6 %copy-start.5 = (f32[4096,448]{0,1:T(8,128)S(1)}, f32[4096,448]{0,1:T(8,128)}, u32[]{:S(2)}) copy-start(f32[4096,448]{0,1:T(8,128)} %param.13) | copy-start | bytes 22020100
  14.3 7.1 %collective-permute-start = (bf16[4,128,128]{2,1,0:T(8,128)(2,1)S(1)}, bf16[4,128,128]{2,1,0:T(8,128)(2,1)S(1)}, u32[]{:S(2)}, u32[]{:S(2)}) collective-permute-start(bf16[4,128,128]{2,1,0:T(8,128)(2,1)S(1)} %get-tuple-element.75), channel_id=1, source_target_pairs={{0,4},{1,5},{2,6},{3,7},{4,0},{5,1},{6,2},{7,3},{8,12},{9,13},{10,... | collective-permute-start | bytes 393224 | tf_op jit(solution)/shard_map/ppermute | solution.py:33
  17.5 11.4 %collective-permute-start.2 = (bf16[8,18432]{1,0:T(8,128)(2,1)S(1)}, bf16[8,18432]{1,0:T(8,128)(2,1)}, u32[]{:S(2)}, u32[]{:S(2)}) collective-permute-start(bf16[8,18432]{1,0:T(8,128)(2,1)S(1)} %pad_maximum_fusion.2), channel_id=1, source_target_pairs={{0,4},{1,5},{2,6},{3,7},{4,0},{5,1},{6,2},{7,3},{8,12},{9,13},{10,... | collective-permute-start | bytes 884744 | tf_op jit(solution)/shard_map/ppermute | solution.py:33
  21.5 13.4 %collective-permute-start.1 = (bf16[512,256]{1,0:T(8,128)(2,1)S(1)}, bf16[512,256]{1,0:T(8,128)(2,1)S(1)}, u32[]{:S(2)}, u32[]{:S(2)}) collective-permute-start(bf16[512,256]{1,0:T(8,128)(2,1)S(1)} %maximum_select_fusion.2), channel_id=1, source_target_pairs={{0,32},{1,97},{2,34},{3,99},{4,36},{5,101},{6,38},{7,103},{8,40},{... | collective-permute-start | bytes 786440 | tf_op jit(solution)/shard_map/ppermute | solution.py:33
  25.3 20.9 %copy-start.11 = (s32[4]{0:T(128)S(1)}, s32[4]{0:T(128)}, u32[]{:S(2)}) copy-start(s32[4]{0:T(128)} %param.16) | copy-start | bytes 52
  25.3 43.9 %collective-permute-start.3 = (bf16[448,2048]{1,0:T(8,128)(2,1)S(1)}, bf16[448,2048]{1,0:T(8,128)(2,1)}, u32[]{:S(2)}, u32[]{:S(2)}) collective-permute-start(bf16[448,2048]{1,0:T(8,128)(2,1)S(1)} %constant_dynamic-slice_fusion.1), channel_id=1, source_target_pairs={{0,6},{1,7},{2,4},{3,5},{4,2},{5,3},{6,0},{7,1},{8,14},{9,15},{10,... | collective-permute-start | bytes 5505032 | tf_op jit(solution)/shard_map/ppermute | solution.py:33
  34.9 0.7 copy-start.6
  36.9 57.5 %copy-start.7 = (bf16[512,256]{1,0:T(8,128)(2,1)S(1)}, bf16[512,256]{1,0:T(8,128)(2,1)}, u32[]{:S(2)}) copy-start(bf16[512,256]{1,0:T(8,128)(2,1)} %copy-done.6) | copy-start | bytes 786436
  37.9 22.5 %all-to-all-start = ((bf16[16,2,8,1152]{3,2,1,0:T(8,128)(2,1)}), bf16[16,2,8,1152]{3,2,1,0:T(8,128)(2,1)S(1)}, u32[]{:S(2)}, u32[]{:S(2)}) async-start(bf16[16,2,8,1152]{3,2,1,0:T(8,128)(2,1)} %copy.46), calls=%async_computation | async-start | bytes 1179648 | tf_op jit(solution)/shard_map/all_to_all | solution.py:268
  44.3 16.1 %collective-permute-start.4 = (bf16[512,256]{1,0:T(8,128)(2,1)}, bf16[512,256]{1,0:T(8,128)(2,1)}, u32[]{:S(2)}, u32[]{:S(2)}) collective-permute-start(bf16[512,256]{1,0:T(8,128)(2,1)} %copy-done.6), channel_id=1, source_target_pairs={{0,32},{1,97},{2,34},{3,99},{4,36},{5,101},{6,38},{7,103},{8,40},{... | collective-permute-start | bytes 786440 | tf_op jit(solution)/shard_map/ppermute | solution.py:33
  69.2 28.5 %collective-permute-start.6 = (bf16[448,2048]{1,0:T(8,128)(2,1)}, bf16[448,2048]{1,0:T(8,128)(2,1)}, u32[]{:S(2)}, u32[]{:S(2)}) collective-permute-start(bf16[448,2048]{1,0:T(8,128)(2,1)} %collective-permute-done.3), channel_id=1, source_target_pairs={{0,1},{1,0},{2,3},{3,2},{4,5},{5,4},{6,7},{7,6},{8,9},{9,8},{10,11... | collective-permute-start | bytes 5505032 | tf_op jit(solution)/shard_map/ppermute | solution.py:33
  69.6 24.8 %collective-permute-start.5 = (bf16[512,256]{1,0:T(8,128)(2,1)}, bf16[512,256]{1,0:T(8,128)(2,1)S(1)}, u32[]{:S(2)}, u32[]{:S(2)}) collective-permute-start(bf16[512,256]{1,0:T(8,128)(2,1)} %collective-permute-done.4), channel_id=1, source_target_pairs={{0,32},{1,97},{2,34},{3,99},{4,36},{5,101},{6,38},{7,103},{8,40},{... | collective-permute-start | bytes 786440 | tf_op jit(solution)/shard_map/ppermute | solution.py:33
  69.7 76.5 %collective-permute-start.8 = (bf16[3584,448]{0,1:T(8,128)(2,1)}, bf16[3584,448]{0,1:T(8,128)(2,1)}, u32[]{:S(2)}, u32[]{:S(2)}) collective-permute-start(bf16[3584,448]{0,1:T(8,128)(2,1)} %param.11), channel_id=1, source_target_pairs={{0,4},{1,5},{2,6},{3,7},{4,0},{5,1},{6,2},{7,3},{8,12},{9,13},{10,... | collective-permute-start | bytes 9633800 | tf_op jit(solution)/shard_map/ppermute | solution.py:33
  73.7 19.7 %all-to-all-start.1 = ((bf16[16,4,8,256]{3,2,1,0:T(8,128)(2,1)}), bf16[16,4,8,256]{3,2,1,0:T(8,128)(2,1)S(1)}, u32[]{:S(2)}, u32[]{:S(2)}) async-start(bf16[16,4,8,256]{3,2,1,0:T(8,128)(2,1)} %broadcast_in_dim.91), calls=%async_computation.1 | async-start | bytes 524288 | tf_op jit(solution)/shard_map/all_to_all | solution.py:273
  95.5 33.4 %collective-permute-start.7 = (bf16[4,512,256]{2,1,0:T(8,128)(2,1)S(1)}, bf16[4,512,256]{2,1,0:T(8,128)(2,1)S(1)}, u32[]{:S(2)}, u32[]{:S(2)}) collective-permute-start(bf16[4,512,256]{2,1,0:T(8,128)(2,1)S(1)} %pad_maximum_fusion.1.refs_0_), channel_id=1, source_target_pairs={{0,8},{1,25},{2,10},{3,27},{4,12},{5,29},{6,14},{7,31},{8,16},{9,1... | collective-permute-start | bytes 3145736 | tf_op jit(solution)/shard_map/ppermute | solution.py:33
  97.6 3.4 %copy-start.2 = (bf16[448,4096]{1,0:T(8,128)(2,1)S(1)}, bf16[448,4096]{1,0:T(8,128)(2,1)}, u32[]{:S(2)}) copy-start(bf16[448,4096]{1,0:T(8,128)(2,1)} %fusion.refs_0_.refs_1_.refs_2_.refs_3_) | copy-start | bytes 11010052
  117.1 12.0 %copy-start.10 = (s32[32,4]{0,1:T(4,128)S(1)}, s32[32,4]{0,1:T(4,128)}, u32[]{:S(2)}) copy-start(s32[32,4]{0,1:T(4,128)} %param.17) | copy-start | bytes 1540
  126.0 1.9 copy-start.3
  128.9 17.3 %collective-permute-start.9 = (bf16[4,512,256]{2,1,0:T(8,128)(2,1)S(1)}, bf16[4,512,256]{2,1,0:T(8,128)(2,1)S(1)}, u32[]{:S(2)}, u32[]{:S(2)}) collective-permute-start(bf16[4,512,256]{2,1,0:T(8,128)(2,1)S(1)} %collective-permute-done.7.refs_0_), channel_id=1, source_target_pairs={{0,8},{1,25},{2,10},{3,27},{4,12},{5,29},{6,14},{7,31},{8,16},{9,1... | collective-permute-start | bytes 3145736 | tf_op jit(solution)/shard_map/ppermute | solution.py:33
  146.2 16.1 %collective-permute-start.10 = (bf16[4,512,256]{2,1,0:T(8,128)(2,1)S(1)}, bf16[4,512,256]{2,1,0:T(8,128)(2,1)S(1)}, u32[]{:S(2)}, u32[]{:S(2)}) collective-permute-start(bf16[4,512,256]{2,1,0:T(8,128)(2,1)S(1)} %collective-permute-done.9.refs_1_), channel_id=1, source_target_pairs={{0,8},{1,25},{2,10},{3,27},{4,12},{5,29},{6,14},{7,31},{8,16},{9,1... | collective-permute-start | bytes 3145736 | tf_op jit(solution)/shard_map/ppermute | solution.py:33
  147.1 8.7 %collective-permute-start.11 = (bf16[512,448]{1,0:T(8,128)(2,1)S(1)}, bf16[512,448]{1,0:T(8,128)(2,1)S(1)}, u32[]{:S(2)}, u32[]{:S(2)}) collective-permute-start(bf16[512,448]{1,0:T(8,128)(2,1)S(1)} %get-tuple-element.50), channel_id=1, source_target_pairs={{0,1},{1,0},{2,3},{3,2},{4,5},{5,4},{6,7},{7,6},{8,9},{9,8},{10,11... | collective-permute-start | bytes 1376264 | tf_op jit(solution)/shard_map/ppermute | solution.py:33
  147.1 23.9 %collective-permute-start.13 = (bf16[512,448]{1,0:T(8,128)(2,1)S(1)}, bf16[512,448]{1,0:T(8,128)(2,1)S(1)}, u32[]{:S(2)}, u32[]{:S(2)}) collective-permute-start(bf16[512,448]{1,0:T(8,128)(2,1)S(1)} %get-tuple-element.54), channel_id=1, source_target_pairs={{0,1},{1,0},{2,3},{3,2},{4,5},{5,4},{6,7},{7,6},{8,9},{9,8},{10,11... | collective-permute-start | bytes 1376264 | tf_op jit(solution)/shard_map/ppermute | solution.py:33
  155.9 34.1 %collective-permute-start.15 = (bf16[512,448]{1,0:T(8,128)(2,1)S(1)}, bf16[512,448]{1,0:T(8,128)(2,1)S(1)}, u32[]{:S(2)}, u32[]{:S(2)}) collective-permute-start(bf16[512,448]{1,0:T(8,128)(2,1)S(1)} %add_convert_fusion.2), channel_id=1, source_target_pairs={{0,2},{1,3},{2,0},{3,1},{4,6},{5,7},{6,4},{7,5},{8,10},{9,11},{10,... | collective-permute-start | bytes 1376264 | tf_op jit(solution)/shard_map/ppermute | solution.py:33
  162.3 8.9 %collective-permute-start.12 = (bf16[512,448]{1,0:T(8,128)(2,1)S(1)}, bf16[512,448]{1,0:T(8,128)(2,1)S(1)}, u32[]{:S(2)}, u32[]{:S(2)}) collective-permute-start(bf16[512,448]{1,0:T(8,128)(2,1)S(1)} %get-tuple-element.52), channel_id=1, source_target_pairs={{0,1},{1,0},{2,3},{3,2},{4,5},{5,4},{6,7},{7,6},{8,9},{9,8},{10,11... | collective-permute-start | bytes 1376264 | tf_op jit(solution)/shard_map/ppermute | solution.py:33
  170.4 2.6 %copy-start.4 = (bf16[2,4,512,448]{3,2,1,0:T(8,128)(2,1)S(1)}, bf16[2,4,512,448]{3,2,1,0:T(8,128)(2,1)}, u32[]{:S(2)}) copy-start(bf16[2,4,512,448]{3,2,1,0:T(8,128)(2,1)} %copy-done.3) | copy-start | bytes 11010052
  170.4 2.4 %collective-permute-start.14 = (bf16[512,448]{1,0:T(8,128)(2,1)S(1)}, bf16[512,448]{1,0:T(8,128)(2,1)S(1)}, u32[]{:S(2)}, u32[]{:S(2)}) collective-permute-start(bf16[512,448]{1,0:T(8,128)(2,1)S(1)} %slice_bitcast_fusion), channel_id=1, source_target_pairs={{0,1},{1,0},{2,3},{3,2},{4,5},{5,4},{6,7},{7,6},{8,9},{9,8},{10,11... | collective-permute-start | bytes 1376264 | tf_op jit(solution)/shard_map/ppermute | solution.py:33
  171.3 18.7 %collective-permute-start.16 = (bf16[512,448]{1,0:T(8,128)(2,1)S(1)}, bf16[512,448]{1,0:T(8,128)(2,1)S(1)}, u32[]{:S(2)}, u32[]{:S(2)}) collective-permute-start(bf16[512,448]{1,0:T(8,128)(2,1)S(1)} %add_convert_fusion.1), channel_id=1, source_target_pairs={{0,2},{1,3},{2,0},{3,1},{4,6},{5,7},{6,4},{7,5},{8,10},{9,11},{10,... | collective-permute-start | bytes 1376264 | tf_op jit(solution)/shard_map/ppermute | solution.py:33
  173.0 39.2 %copy-start.1 = (bf16[4096,128]{1,0:T(8,128)(2,1)S(1)}, bf16[4096,128]{1,0:T(8,128)(2,1)}, u32[]{:S(2)}) copy-start(bf16[4096,128]{1,0:T(8,128)(2,1)} %param.12) | copy-start | bytes 3145732
  192.6 18.3 %all-to-all-start.2 = ((f32[32,4,128]{2,1,0:T(4,128)}), f32[32,4,128]{2,1,0:T(4,128)S(1)}, u32[]{:S(2)}, u32[]{:S(2)}) async-start(f32[32,4,128]{2,1,0:T(4,128)} %bitcast_select_fusion), calls=%async_computation.2 | async-start | bytes 131072 | tf_op jit(solution)/shard_map/all_to_all | solution.py:352
Sparse Core Ops, SparseCore 0:
  10.2 117.0 all-gather.1
where the time goes:
time: 220 us; the launch traced here: 219 us
  Pallas kernels  74.4 us (34%)
  waiting for transfers between devices  55.8 us (25%)
  starting transfers between devices  42 us (19%)
  between operations  14.6 us (7%)
  local copies, waits for them, and re-layouts  13.9 us (6%)
  other arithmetic  12.4 us (6%)
  matrix products  5.86 us (3%)
    ppermute x17, waiting for transfers between devices, send(): return lax.ppermute(value, AXES, pairs)  35.2 us
    pallas_call x3, Pallas kernels, products_of(): pl.pallas_call(products_kernel, grid_spec=pltpu.PrefetchScalarGridSpec(nu...  30.6 us
    pallas_call x2, Pallas kernels, mixed_of(): pl.pallas_call(functools.partial(mixed_kernel, chunks), grid=(2, queries)...  25.9 us
    ppermute x17, starting transfers between devices, send(): return lax.ppermute(value, AXES, pairs)  19.6 us
    pallas_call x1, Pallas kernels, precond_of(): pl.pallas_call(precond_kernel, grid_spec=pltpu.PrefetchScalarGridSpec(num...  16.1 us
    all_to_all x1, waiting for transfers between devices, per_device(): lax.all_to_all(jnp.broadcast_to(owned[None, ..., 2 * width:], (16, querie...  11.4 us
    all_to_all x1, waiting for transfers between devices, per_device(): terms = lax.all_to_all(full, ex, 0, 0, tiled=True)  8.56 us
    all_to_all x1, starting transfers between devices, per_device(): terms = lax.all_to_all(full, ex, 0, 0, tiled=True)  8.39 us
  transfers between devices with their start and end apart: 21, of which 8 were waited for; matrix products, arithmetic and copies ran while one was open for 12% of the time, Pallas kernels for 33%

commit v1 on v0

--- a/solution.py
+++ b/solution.py
@@ -182,7 +182,7 @@
             transcendentals=0,
         ),
     )(z_blocks, gathered, basis)
-    return [out[g] for g in range(groups)]
+    return out
 
 
 def score_kernel(mixed, stay, stay_far, arrived, arrived_far, out):
@@ -322,20 +322,17 @@
             for a, b in zip(one, two)
         ]
 
-    z_blocks = 2 * jnp.stack([1 - xl, 1 - xl, xl, xl]) + jnp.stack([1 - c, c] * 2)
+    z_blocks = 2 * jnp.stack([1 - xl, xl] * 2) + jnp.stack([1 - c, 1 - c, c, c])
     z_blocks = z_blocks.astype(jnp.int32)
     made = products_of(z_blocks, gathered, hidden_basis.T)
     made, basis_far, steps[2] = lax.optimization_barrier((made, basis_far, steps[2]))
     steps.append(send(steps[2], RING_Y))
-    made_far = products_of(z_blocks[:2], gathered, basis_far.T)
-    made_far, steps[3], gathered = lax.optimization_barrier(
-        (made_far, steps[3], gathered)
-    )
-    made_far += products_of(z_blocks[2:], gathered, basis_far.T)
-    there, here, there_last, here_last = zip(made, made_far)
-    leave = total(here, swapped(there, OTHER_CORE))
+    far = products_of(z_blocks[:2], gathered, basis_far.T)
+    far, steps[3], gathered = lax.optimization_barrier((far, steps[3], gathered))
+    here = [made[2:], products_of(z_blocks[2:], gathered, basis_far.T)]
+    both = total(here, swapped([made[:2], far], OTHER_CORE))
+    leave, stay = ([v[g] for v in both] for g in range(2))
     arrived = swapped(leave, OTHER_XL)
-    stay = total(here_last, swapped(there_last, OTHER_CORE))
     steps[3], early, leave, stay = lax.optimization_barrier(
         (steps[3], early, leave, stay)
     )

time: 220 us -> 228 us (1.036)
  local copies, waits for them, and re-layouts: 13.9 us -> 23.4 us
  starting transfers between devices: 42 us -> 38.7 us
  other arithmetic: 12.4 us -> 15 us
    slice x1 -> x3, local copies, waits for them, and re-layouts: 0.07 us -> 4.93 us  [the longest x2 4.86 us: per_device(): both = total(here, swapped([made[:2], far], OTHER_CORE))]
    ppermute x0 -> x2, local copies, waits for them, and re-layouts: none -> 3.71 us  [send(): return lax.ppermute(value, AXES, pairs)]
    ppermute x17 -> x15, starting transfers between devices: 19.6 us -> 16.9 us  [send(): return lax.ppermute(value, AXES, pairs)]
    convert_element_type x4 -> x2, other arithmetic: 0.54 us -> 3.18 us  [total(): (a.astype(jnp.float32) + b.astype(jnp.float32)).astype(jnp.bfloat16)]
    ppermute x17 -> x15, waiting for transfers between devices: 35.2 us -> 33.9 us  [send(): return lax.ppermute(value, AXES, pairs)]
    unnamed x27 -> x31, local copies, waits for them, and re-layouts: 4.62 us -> 5.05 us
  transfers between devices with their start and end apart: 21 -> 19, of which waited for: 8 -> 9; matrix products, arithmetic and copies ran while one was open for 12% -> 17% of each run, Pallas kernels for 33% -> 32%
where the time goes in v1:
time: 228 us; the launch traced here: 227 us
  Pallas kernels  75 us (33%)
  waiting for transfers between devices  54.5 us (24%)
  starting transfers between devices  38.7 us (17%)
  local copies, waits for them, and re-layouts  23.4 us (10%)
  other arithmetic  15 us (7%)
  between operations  14.5 us (6%)
  matrix products  5.86 us (3%)
    ppermute x15, waiting for transfers between devices, send(): return lax.ppermute(value, AXES, pairs)  33.9 us
    pallas_call x3, Pallas kernels, products_of(): pl.pallas_call(products_kernel, grid_spec=pltpu.PrefetchScalarGridSpec(nu...  30.6 us
    pallas_call x2, Pallas kernels, mixed_of(): pl.pallas_call(functools.partial(mixed_kernel, chunks), grid=(2, queries)...  26.5 us
    ppermute x15, starting transfers between devices, send(): return lax.ppermute(value, AXES, pairs)  16.9 us
    pallas_call x1, Pallas kernels, precond_of(): pl.pallas_call(precond_kernel, grid_spec=pltpu.PrefetchScalarGridSpec(num...  16.1 us
    all_to_all x1, waiting for transfers between devices, per_device(): lax.all_to_all(jnp.broadcast_to(owned[None, ..., 2 * width:], (16, querie...  11.4 us
    all_to_all x1, waiting for transfers between devices, per_device(): terms = lax.all_to_all(full, ex, 0, 0, tiled=True)  8.56 us
    all_to_all x1, starting transfers between devices, per_device(): terms = lax.all_to_all(full, ex, 0, 0, tiled=True)  7.8 us
  transfers between devices with their start and end apart: 19, of which 9 were waited for; matrix products, arithmetic and copies ran while one was open for 17% of the time, Pallas kernels for 32%

profile of v1, /device:TPU:0, one launch (start us, length us, event | category | flops | bytes accessed | tf_op | source)
XLA Modules:
  0.0 226.9 jit_solution(13799614733123964451)
XLA Ops:
  7.2 0.7 all-gather.2.cloned.1.call-update
  7.9 0.5 copy-done
  8.4 5.9 %convolution_convert_fusion = bf16[1024,128]{1,0:T(8,128)(2,1)S(1)} fusion(bf16[1024,4096]{1,0:T(8,128)(2,1)} %param.10, bf16[4096,128]{1,0:T(8,128)(2,1)S(1)} %copy-done), kind=kOutput, calls=%fused_computation.6 | convolution fusion | flops 1073872896 | bytes 9699328 | tf_op jit(solution)/shard_map/dot_general | solution.py:41
  14.3 3.2 %collective-permute-start = (bf16[4,128,128]{2,1,0:T(8,128)(2,1)S(1)}, bf16[4,128,128]{2,1,0:T(8,128)(2,1)S(1)}, u32[]{:S(2)}, u32[]{:S(2)}) collective-permute-start(bf16[4,128,128]{2,1,0:T(8,128)(2,1)S(1)} %get-tuple-element.65), channel_id=1, source_target_pairs={{0,4},{1,5},{2,6},{3,7},{4,0},{5,1},{6,2},{7,3},{8,12},{9,13},{10,... | collective-permute-start | bytes 393224 | tf_op jit(solution)/shard_map/ppermute | solution.py:33
  17.5 0.5 collective-permute-start.2
  18.0 2.8 %fusion.refs_0_.refs_1_.refs_2_.refs_3_ = bf16[448,4096]{1,0:T(8,128)(2,1)} fusion(f32[4096,448]{0,1:T(8,128)S(1)} %copy-done.7), kind=kLoop, calls=%fused_computation.3 | loop fusion | flops 5505024 | bytes 11010048 | tf_op jit(solution)/shard_map/convert_element_type | solution.py:246
  20.8 0.6 collective-permute-done
  21.5 2.0 collective-permute-start.1
  23.5 1.8 constant_dynamic-slice_fusion.1
  25.3 3.6 %collective-permute-start.3 = (bf16[448,2048]{1,0:T(8,128)(2,1)S(1)}, bf16[448,2048]{1,0:T(8,128)(2,1)}, u32[]{:S(2)}, u32[]{:S(2)}) collective-permute-start(bf16[448,2048]{1,0:T(8,128)(2,1)S(1)} %constant_dynamic-slice_fusion.1), channel_id=1, source_target_pairs={{0,6},{1,7},{2,4},{3,5},{4,2},{5,3},{6,0},{7,1},{8,14},{9,15},{10,... | collective-permute-start | bytes 5505032 | tf_op jit(solution)/shard_map/ppermute | solution.py:33
  28.9 6.0 %collective-permute-done.1 = bf16[512,256]{1,0:T(8,128)(2,1)S(1)} collective-permute-done((bf16[512,256]{1,0:T(8,128)(2,1)S(1)}, bf16[512,256]{1,0:T(8,128)(2,1)S(1)}, u32[]{:S(2)}, u32[]{:S(2)}) %collective-permute-start.1) | collective-permute-done | bytes 262176 | tf_op jit(solution)/shard_map/ppermute | solution.py:33
  34.9 0.7 copy-done.9
  35.6 1.2 maximum_select_fusion
  37.0 0.9 copy.54
  37.9 6.4 %all-to-all-start = ((bf16[16,2,8,1152]{3,2,1,0:T(8,128)(2,1)}), bf16[16,2,8,1152]{3,2,1,0:T(8,128)(2,1)S(1)}, u32[]{:S(2)}, u32[]{:S(2)}) async-start(bf16[16,2,8,1152]{3,2,1,0:T(8,128)(2,1)} %copy.54), calls=%async_computation | async-start | bytes 1179648 | tf_op jit(solution)/shard_map/all_to_all | solution.py:268
  44.4 1.9 collective-permute-start.4
  46.2 14.1 %collective-permute-done.4 = bf16[512,256]{1,0:T(8,128)(2,1)S(1)} collective-permute-done((bf16[512,256]{1,0:T(8,128)(2,1)}, bf16[512,256]{1,0:T(8,128)(2,1)S(1)}, u32[]{:S(2)}, u32[]{:S(2)}) %collective-permute-start.4) | collective-permute-done | bytes 262176 | tf_op jit(solution)/shard_map/ppermute | solution.py:33
  60.3 8.9 %collective-permute-done.3 = bf16[448,2048]{1,0:T(8,128)(2,1)} collective-permute-done((bf16[448,2048]{1,0:T(8,128)(2,1)S(1)}, bf16[448,2048]{1,0:T(8,128)(2,1)}, u32[]{:S(2)}, u32[]{:S(2)}) %collective-permute-start.3) | collective-permute-done | bytes 1835040 | tf_op jit(solution)/shard_map/ppermute | solution.py:33
  69.2 2.0 collective-permute-start.8
  71.5 0.8 collective-permute-start.5
  72.3 0.6 gather_fusion
  73.0 0.7 broadcast_in_dim.91
  73.7 7.6 %all-to-all-start.1 = ((bf16[16,4,8,256]{3,2,1,0:T(8,128)(2,1)}), bf16[16,4,8,256]{3,2,1,0:T(8,128)(2,1)S(1)}, u32[]{:S(2)}, u32[]{:S(2)}) async-start(bf16[16,4,8,256]{3,2,1,0:T(8,128)(2,1)} %broadcast_in_dim.91), calls=%async_computation.1 | async-start | bytes 524288 | tf_op jit(solution)/shard_map/all_to_all | solution.py:273
  81.5 0.1 reshape.123
  81.6 0.4 rev.3
  82.1 11.4 %all-to-all-done.1 = bf16[16,4,8,256]{3,2,1,0:T(8,128)(2,1)S(1)} async-done(((bf16[16,4,8,256]{3,2,1,0:T(8,128)(2,1)}), bf16[16,4,8,256]{3,2,1,0:T(8,128)(2,1)S(1)}, u32[]{:S(2)}, u32[]{:S(2)}) %all-to-all-start.1) | async-done | bytes 262176 | tf_op jit(solution)/shard_map/all_to_all | solution.py:273
  93.5 0.1 copy.76
  93.6 0.8 copy.71
  94.4 1.1 pad_maximum_fusion.1.refs_0_
  95.5 0.6 collective-permute-start.7
  96.3 1.4 copy.57.refs_8_.refs_9_.refs_10_.refs_11_
  97.7 2.8 %pad_maximum_fusion.refs_4_.refs_5_.refs_6_.refs_7_ = bf16[448,4096]{1,0:T(8,128)(2,1)S(1)} fusion(bf16[448,2048]{1,0:T(8,128)(2,1)} %collective-permute-done.6, bf16[448,2048]{1,0:T(8,128)(2,1)} %collective-permute-done.3), kind=kLoop, calls=%fused_computation.2 | loop fusion | flops 7340032 | bytes 7340032 | tf_op jit(solution)/shard_map/concatenate | solution.py:295
  100.5 0.6 copy-done.2
  101.1 16.1 %shard_map.104.refs_1_.refs_3_.refs_4_.refs_5_ = bf16[2,4,4096,448]{3,2,1,0:T(8,128)(2,1)} custom-call(s32[32]{0:T(128)S(1)} %concatenate.61.at, bf16[448,4096]{1,0:T(8,128)(2,1)S(1)} %copy-done.2, bf16[448,4096]{1,0:T(8,128)(2,1)S(1)} %copy-done.2, bf16[448,4096]{1,0:T(8,128)(2,1)S(1)} %copy-done.2, bf16[448,4096]{1,0:T(8,128)(2,1)S(1)} %copy-done.2, ...), custom_call_target="tpu_custom_call" | custom-call | flops 939524096 | bytes 80000000 | tf_op jit(solution)/shard_map/pallas_call | solution.py:70
  117.2 8.9 %shard_map.105.refs_6_ = bf16[2,4,512,448]{3,2,1,0:T(8,128)(2,1)S(1)} custom-call(bf16[4,512,256]{2,1,0:T(8,128)(2,1)S(1)} %pad_maximum_fusion.1.refs_0_, bf16[2,4,4096,448]{3,2,1,0:T(8,128)(2,1)} %shard_map.104.refs_1_.refs_3_.refs_4_.refs_5_), custom_call_target="tpu_custom_call" | custom-call | flops 3758096384 | bytes 10000000 | tf_op jit(solution)/shard_map/pallas_call | solution.py:126
  126.1 1.9 copy-done.3
  128.0 0.9 collective-permute-done.7.refs_0_
  128.9 14.5 %shard_map.106 = bf16[4,512,448]{2,1,0:T(8,128)(2,1)} custom-call(s32[4]{0:T(128)S(1)} %fusion.7.at, bf16[2048,3584]{1,0:T(8,128)(2,1)} %all-gather.2.cloned.1.call-done.rows, bf16[448,3584]{1,0:T(8,128)(2,1)} %bitcast.87), custom_call_target="tpu_custom_call" | custom-call | flops 6576668672 | bytes 16000000 | tf_op jit(solution)/shard_map/pallas_call | solution.py:164
  143.5 1.4 collective-permute-done.9.refs_1_
  144.9 2.7 %slice.42 = bf16[2,512,448]{2,1,0:T(8,128)(2,1)} slice(bf16[4,512,448]{2,1,0:T(8,128)(2,1)} %shard_map.106), slice={[0:2], [0:512], [0:448]} | slice | bytes 1835008 | tf_op jit(solution)/shard_map/slice | solution.py:333
  147.5 2.2 copy.61
  149.7 0.2 collective-permute-start.11
  150.0 0.2 dynamic-slice_reduce_fusion
  150.2 0.6 fusion.3
  150.9 8.1 %shard_map.107 = bf16[2,512,448]{2,1,0:T(8,128)(2,1)S(1)} custom-call(s32[2]{0:T(128)S(1)} %get-tuple-element.67.at, bf16[2048,3584]{1,0:T(8,128)(2,1)} %all-gather.2.cloned.1.call-done.rows, bf16[448,3584]{1,0:T(8,128)(2,1)} %bitcast.24.basis), custom_call_target="tpu_custom_call" | custom-call | flops 3288334336 | bytes 8000000 | tf_op jit(solution)/shard_map/pallas_call | solution.py:164
  158.9 2.0 collective-permute-done.10.refs_2_
  161.0 1.3 copy.63
  162.5 1.5 copy.62
  163.9 1.5 add_convert_fusion.1
  165.4 0.9 slice_bitcast_fusion.1
  166.3 1.5 collective-permute-start.13
  167.8 8.1 %shard_map.108 = bf16[2,512,448]{2,1,0:T(8,128)(2,1)S(1)} custom-call(s32[2]{0:T(128)S(1)} %get-tuple-element.66.at, bf16[2048,3584]{1,0:T(8,128)(2,1)} %all-gather.2.cloned.1.call-done.rows, bf16[448,3584]{1,0:T(8,128)(2,1)} %bitcast.24.basis), custom_call_target="tpu_custom_call" | custom-call | flops 3288334336 | bytes 8000000 | tf_op jit(solution)/shard_map/pallas_call | solution.py:164
  175.9 2.2 copy.64
  178.1 1.7 add_convert_fusion
  179.9 0.6 collective-permute-start.14
  180.6 0.3 copy-done.6
  180.9 17.6 %shard_map.109.mixed = bf16[2,4,512,448]{3,2,1,0:T(8,128)(2,1)S(1)} custom-call(bf16[4,512,256]{2,1,0:T(8,128)(2,1)S(1)} %collective-permute-done.7.refs_0_, bf16[4,512,256]{2,1,0:T(8,128)(2,1)S(1)} %copy-done.6, bf16[4,512,256]{2,1,0:T(8,128)(2,1)} %collective-permute-done.10.refs_2_, bf16[2,4,4096,448]{3,2,1,0:T(8,128)(2,1)} %shard_map.104.refs_1_.refs_3_.refs_4_.refs_5_, ...), custom_call_target="tpu_custom_call" | custom-call | flops 11274289152 | bytes 30000000 | tf_op jit(solution)/shard_map/pallas_call | solution.py:126
  198.6 1.8 shard_map.110
  200.3 0.7 bitcast_select_fusion
  201.1 7.8 %all-to-all-start.2 = ((f32[32,4,128]{2,1,0:T(4,128)}), f32[32,4,128]{2,1,0:T(4,128)S(1)}, u32[]{:S(2)}, u32[]{:S(2)}) async-start(f32[32,4,128]{2,1,0:T(4,128)} %bitcast_select_fusion), calls=%async_computation.2 | async-start | bytes 131072 | tf_op jit(solution)/shard_map/all_to_all | solution.py:349
  208.9 1.3 compare_and_fusion
  210.2 8.6 %all-to-all-done.2 = f32[32,4,128]{2,1,0:T(4,128)S(1)} async-done(((f32[32,4,128]{2,1,0:T(4,128)}), f32[32,4,128]{2,1,0:T(4,128)S(1)}, u32[]{:S(2)}, u32[]{:S(2)}) %all-to-all-start.2) | async-done | bytes 65568 | tf_op jit(solution)/shard_map/all_to_all | solution.py:349
  218.8 0.6 select_reduce_fusion
  219.4 0.6 constant_dynamic-slice_fusion
  (71 shorter events, 1.7 us)
Async XLA Ops:
  7.2 1.2 copy-start
  7.2 121.8 %all-gather.2.cloned.1.call-start = ((), (), s32[]{:S(2)}) async-start(), calls=%async_computation.3 | async-start | bytes 15597568 | tf_op jit(solution)/shard_map/all_gather | solution.py:245
  8.4 9.1 %copy-start.10 = (bf16[1,8,14336]{2,1,0:T(8,128)(2,1)S(1)}, bf16[1,8,14336]{2,1,0:T(8,128)(2,1)}, u32[]{:S(2)}) copy-start(bf16[1,8,14336]{2,1,0:T(8,128)(2,1)} %param.14) | copy-start | bytes 688132
  8.4 9.1 %copy-start.11 = (bf16[1,8,4096]{2,1,0:T(8,128)(2,1)S(1)}, bf16[1,8,4096]{2,1,0:T(8,128)(2,1)}, u32[]{:S(2)}) copy-start(bf16[1,8,4096]{2,1,0:T(8,128)(2,1)} %param.15) | copy-start | bytes 196612
  8.4 9.6 %copy-start.7 = (f32[4096,448]{0,1:T(8,128)S(1)}, f32[4096,448]{0,1:T(8,128)}, u32[]{:S(2)}) copy-start(f32[4096,448]{0,1:T(8,128)} %param.13) | copy-start | bytes 22020100
  14.3 7.1 %collective-permute-start = (bf16[4,128,128]{2,1,0:T(8,128)(2,1)S(1)}, bf16[4,128,128]{2,1,0:T(8,128)(2,1)S(1)}, u32[]{:S(2)}, u32[]{:S(2)}) collective-permute-start(bf16[4,128,128]{2,1,0:T(8,128)(2,1)S(1)} %get-tuple-element.65), channel_id=1, source_target_pairs={{0,4},{1,5},{2,6},{3,7},{4,0},{5,1},{6,2},{7,3},{8,12},{9,13},{10,... | collective-permute-start | bytes 393224 | tf_op jit(solution)/shard_map/ppermute | solution.py:33
  17.5 11.4 %collective-permute-start.2 = (bf16[8,18432]{1,0:T(8,128)(2,1)S(1)}, bf16[8,18432]{1,0:T(8,128)(2,1)S(1)}, u32[]{:S(2)}, u32[]{:S(2)}) collective-permute-start(bf16[8,18432]{1,0:T(8,128)(2,1)S(1)} %pad_maximum_fusion.2), channel_id=1, source_target_pairs={{0,4},{1,5},{2,6},{3,7},{4,0},{5,1},{6,2},{7,3},{8,12},{9,13},{10,... | collective-permute-start | bytes 884744 | tf_op jit(solution)/shard_map/ppermute | solution.py:33
  21.5 13.4 %collective-permute-start.1 = (bf16[512,256]{1,0:T(8,128)(2,1)S(1)}, bf16[512,256]{1,0:T(8,128)(2,1)S(1)}, u32[]{:S(2)}, u32[]{:S(2)}) collective-permute-start(bf16[512,256]{1,0:T(8,128)(2,1)S(1)} %maximum_select_fusion.2), channel_id=1, source_target_pairs={{0,32},{1,97},{2,34},{3,99},{4,36},{5,101},{6,38},{7,103},{8,40},{... | collective-permute-start | bytes 786440 | tf_op jit(solution)/shard_map/ppermute | solution.py:33
  25.3 20.9 %copy-start.13 = (s32[4]{0:T(128)S(1)}, s32[4]{0:T(128)}, u32[]{:S(2)}) copy-start(s32[4]{0:T(128)} %param.16) | copy-start | bytes 52
  25.3 43.9 %collective-permute-start.3 = (bf16[448,2048]{1,0:T(8,128)(2,1)S(1)}, bf16[448,2048]{1,0:T(8,128)(2,1)}, u32[]{:S(2)}, u32[]{:S(2)}) collective-permute-start(bf16[448,2048]{1,0:T(8,128)(2,1)S(1)} %constant_dynamic-slice_fusion.1), channel_id=1, source_target_pairs={{0,6},{1,7},{2,4},{3,5},{4,2},{5,3},{6,0},{7,1},{8,14},{9,15},{10,... | collective-permute-start | bytes 5505032 | tf_op jit(solution)/shard_map/ppermute | solution.py:33
  28.9 6.0 %copy-start.8 = (bf16[8,18432]{1,0:T(8,128)(2,1)}, bf16[8,18432]{1,0:T(8,128)(2,1)S(1)}, u32[]{:S(2)}) copy-start(bf16[8,18432]{1,0:T(8,128)(2,1)S(1)} %collective-permute-done.2) | copy-start | bytes 884740
  34.9 0.7 copy-start.9
  37.9 22.4 %all-to-all-start = ((bf16[16,2,8,1152]{3,2,1,0:T(8,128)(2,1)}), bf16[16,2,8,1152]{3,2,1,0:T(8,128)(2,1)S(1)}, u32[]{:S(2)}, u32[]{:S(2)}) async-start(bf16[16,2,8,1152]{3,2,1,0:T(8,128)(2,1)} %copy.54), calls=%async_computation | async-start | bytes 1179648 | tf_op jit(solution)/shard_map/all_to_all | solution.py:268
  44.4 16.0 %collective-permute-start.4 = (bf16[512,256]{1,0:T(8,128)(2,1)}, bf16[512,256]{1,0:T(8,128)(2,1)S(1)}, u32[]{:S(2)}, u32[]{:S(2)}) collective-permute-start(bf16[512,256]{1,0:T(8,128)(2,1)} %copy-done.9), channel_id=1, source_target_pairs={{0,32},{1,97},{2,34},{3,99},{4,36},{5,101},{6,38},{7,103},{8,40},{... | collective-permute-start | bytes 786440 | tf_op jit(solution)/shard_map/ppermute | solution.py:33
  69.2 28.5 %collective-permute-start.6 = (bf16[448,2048]{1,0:T(8,128)(2,1)}, bf16[448,2048]{1,0:T(8,128)(2,1)}, u32[]{:S(2)}, u32[]{:S(2)}) collective-permute-start(bf16[448,2048]{1,0:T(8,128)(2,1)} %collective-permute-done.3), channel_id=1, source_target_pairs={{0,1},{1,0},{2,3},{3,2},{4,5},{5,4},{6,7},{7,6},{8,9},{9,8},{10,11... | collective-permute-start | bytes 5505032 | tf_op jit(solution)/shard_map/ppermute | solution.py:33
  69.2 75.6 %collective-permute-start.8 = (bf16[3584,448]{0,1:T(8,128)(2,1)}, bf16[3584,448]{0,1:T(8,128)(2,1)}, u32[]{:S(2)}, u32[]{:S(2)}) collective-permute-start(bf16[3584,448]{0,1:T(8,128)(2,1)} %param.11), channel_id=1, source_target_pairs={{0,4},{1,5},{2,6},{3,7},{4,0},{5,1},{6,2},{7,3},{8,12},{9,13},{10,... | collective-permute-start | bytes 9633800 | tf_op jit(solution)/shard_map/ppermute | solution.py:33
  71.5 22.9 %collective-permute-start.5 = (bf16[512,256]{1,0:T(8,128)(2,1)S(1)}, bf16[512,256]{1,0:T(8,128)(2,1)S(1)}, u32[]{:S(2)}, u32[]{:S(2)}) collective-permute-start(bf16[512,256]{1,0:T(8,128)(2,1)S(1)} %collective-permute-done.4), channel_id=1, source_target_pairs={{0,32},{1,97},{2,34},{3,99},{4,36},{5,101},{6,38},{7,103},{8,40},{... | collective-permute-start | bytes 786440 | tf_op jit(solution)/shard_map/ppermute | solution.py:33
  73.7 19.7 %all-to-all-start.1 = ((bf16[16,4,8,256]{3,2,1,0:T(8,128)(2,1)}), bf16[16,4,8,256]{3,2,1,0:T(8,128)(2,1)S(1)}, u32[]{:S(2)}, u32[]{:S(2)}) async-start(bf16[16,4,8,256]{3,2,1,0:T(8,128)(2,1)} %broadcast_in_dim.91), calls=%async_computation.1 | async-start | bytes 524288 | tf_op jit(solution)/shard_map/all_to_all | solution.py:273
  95.5 33.3 %collective-permute-start.7 = (bf16[4,512,256]{2,1,0:T(8,128)(2,1)S(1)}, bf16[4,512,256]{2,1,0:T(8,128)(2,1)S(1)}, u32[]{:S(2)}, u32[]{:S(2)}) collective-permute-start(bf16[4,512,256]{2,1,0:T(8,128)(2,1)S(1)} %pad_maximum_fusion.1.refs_0_), channel_id=1, source_target_pairs={{0,8},{1,25},{2,10},{3,27},{4,12},{5,29},{6,14},{7,31},{8,16},{9,1... | collective-permute-start | bytes 3145736 | tf_op jit(solution)/shard_map/ppermute | solution.py:33
  97.7 3.4 %copy-start.2 = (bf16[448,4096]{1,0:T(8,128)(2,1)S(1)}, bf16[448,4096]{1,0:T(8,128)(2,1)}, u32[]{:S(2)}) copy-start(bf16[448,4096]{1,0:T(8,128)(2,1)} %fusion.refs_0_.refs_1_.refs_2_.refs_3_) | copy-start | bytes 11010052
  126.1 1.9 copy-start.3
  128.9 16.0 %collective-permute-start.9 = (bf16[4,512,256]{2,1,0:T(8,128)(2,1)S(1)}, bf16[4,512,256]{2,1,0:T(8,128)(2,1)S(1)}, u32[]{:S(2)}, u32[]{:S(2)}) collective-permute-start(bf16[4,512,256]{2,1,0:T(8,128)(2,1)S(1)} %collective-permute-done.7.refs_0_), channel_id=1, source_target_pairs={{0,8},{1,25},{2,10},{3,27},{4,12},{5,29},{6,14},{7,31},{8,16},{9,1... | collective-permute-start | bytes 3145736 | tf_op jit(solution)/shard_map/ppermute | solution.py:33
  143.5 6.5 %copy-start.12 = (s32[32,4]{0,1:T(4,128)S(1)}, s32[32,4]{0,1:T(4,128)}, u32[]{:S(2)}) copy-start(s32[32,4]{0,1:T(4,128)} %param.17) | copy-start | bytes 1540
  144.9 14.1 %copy-start.5 = (bf16[4,512,256]{2,1,0:T(8,128)(2,1)}, bf16[4,512,256]{2,1,0:T(8,128)(2,1)S(1)}, u32[]{:S(2)}) copy-start(bf16[4,512,256]{2,1,0:T(8,128)(2,1)S(1)} %collective-permute-done.9.refs_1_) | copy-start | bytes 3145732
  144.9 16.1 %collective-permute-start.10 = (bf16[4,512,256]{2,1,0:T(8,128)(2,1)S(1)}, bf16[4,512,256]{2,1,0:T(8,128)(2,1)}, u32[]{:S(2)}, u32[]{:S(2)}) collective-permute-start(bf16[4,512,256]{2,1,0:T(8,128)(2,1)S(1)} %collective-permute-done.9.refs_1_), channel_id=1, source_target_pairs={{0,8},{1,25},{2,10},{3,27},{4,12},{5,29},{6,14},{7,31},{8,16},{9,1... | collective-permute-start | bytes 3145736 | tf_op jit(solution)/shard_map/ppermute | solution.py:33
  149.7 12.7 %collective-permute-start.11 = (bf16[2,512,448]{1,2,0:T(8,128)(2,1)}, bf16[2,512,448]{1,2,0:T(8,128)(2,1)}, u32[]{:S(2)}, u32[]{:S(2)}) collective-permute-start(bf16[2,512,448]{1,2,0:T(8,128)(2,1)} %copy.61), channel_id=1, source_target_pairs={{0,1},{1,0},{2,3},{3,2},{4,5},{5,4},{6,7},{7,6},{8,9},{9,8},{10,11... | collective-permute-start | bytes 2752520 | tf_op jit(solution)/shard_map/ppermute | solution.py:33
  162.3 13.6 %collective-permute-start.12 = (bf16[2,512,448]{1,2,0:T(8,128)(2,1)}, bf16[2,512,448]{1,2,0:T(8,128)(2,1)}, u32[]{:S(2)}, u32[]{:S(2)}) collective-permute-start(bf16[2,512,448]{1,2,0:T(8,128)(2,1)} %copy.63), channel_id=1, source_target_pairs={{0,1},{1,0},{2,3},{3,2},{4,5},{5,4},{6,7},{7,6},{8,9},{9,8},{10,11... | collective-permute-start | bytes 2752520 | tf_op jit(solution)/shard_map/ppermute | solution.py:33
  166.3 32.2 %collective-permute-start.13 = (bf16[512,448]{1,0:T(8,128)(2,1)}, bf16[512,448]{1,0:T(8,128)(2,1)S(1)}, u32[]{:S(2)}, u32[]{:S(2)}) collective-permute-start(bf16[512,448]{1,0:T(8,128)(2,1)} %get-tuple-element.63), channel_id=1, source_target_pairs={{0,2},{1,3},{2,0},{3,1},{4,6},{5,7},{6,4},{7,5},{8,10},{9,11},{10,... | collective-permute-start | bytes 1376264 | tf_op jit(solution)/shard_map/ppermute | solution.py:33
  178.1 2.5 %copy-start.4 = (bf16[2,4,512,448]{3,2,1,0:T(8,128)(2,1)S(1)}, bf16[2,4,512,448]{3,2,1,0:T(8,128)(2,1)}, u32[]{:S(2)}) copy-start(bf16[2,4,512,448]{3,2,1,0:T(8,128)(2,1)} %copy-done.3) | copy-start | bytes 11010052
  178.1 2.8 %copy-start.6 = (bf16[4,512,256]{2,1,0:T(8,128)(2,1)S(1)}, bf16[4,512,256]{2,1,0:T(8,128)(2,1)}, u32[]{:S(2)}) copy-start(bf16[4,512,256]{2,1,0:T(8,128)(2,1)} %copy-done.5) | copy-start | bytes 3145732
  179.9 18.7 %collective-permute-start.14 = (bf16[512,448]{1,0:T(8,128)(2,1)S(1)}, bf16[512,448]{1,0:T(8,128)(2,1)S(1)}, u32[]{:S(2)}, u32[]{:S(2)}) collective-permute-start(bf16[512,448]{1,0:T(8,128)(2,1)S(1)} %get-tuple-element.61), channel_id=1, source_target_pairs={{0,2},{1,3},{2,0},{3,1},{4,6},{5,7},{6,4},{7,5},{8,10},{9,11},{10,... | collective-permute-start | bytes 1376264 | tf_op jit(solution)/shard_map/ppermute | solution.py:33
  180.9 39.2 %copy-start.1 = (bf16[4096,128]{1,0:T(8,128)(2,1)S(1)}, bf16[4096,128]{1,0:T(8,128)(2,1)}, u32[]{:S(2)}) copy-start(bf16[4096,128]{1,0:T(8,128)(2,1)} %param.12) | copy-start | bytes 3145732
  201.1 17.7 %all-to-all-start.2 = ((f32[32,4,128]{2,1,0:T(4,128)}), f32[32,4,128]{2,1,0:T(4,128)S(1)}, u32[]{:S(2)}, u32[]{:S(2)}) async-start(f32[32,4,128]{2,1,0:T(4,128)} %bitcast_select_fusion), calls=%async_computation.2 | async-start | bytes 131072 | tf_op jit(solution)/shard_map/all_to_all | solution.py:349
Sparse Core Ops, SparseCore 0:
  10.2 117.0 all-gather.1
